TPU v7x, 32 devices: a whole 2x2x4 slice. The times are simulated.
32 devices in a mesh: groups: 2 (over y), rank: 16 (over z, x, core).
Axes of the slice: x: 2, y: 2, z: 4, core: 2. Of those that a mesh axis runs over, the one named last changes fastest.
Arguments:
- pool: bfloat16 [512, 1024], P(('groups', 'rank')), parts along dimension 0, may hold values from -6 to 6
- kv_cache: bfloat16 [128, 4, 64, 256], P(('groups', 'rank')), parts along dimension 0
- w_qu: bfloat16 [1024, 1024], replicated, may hold values from -0.1875 to 0.1875
- w_out: bfloat16 [512, 1024], replicated, may hold values from -0.25 to 0.25
- norm_gain: float32 [512], replicated, may hold values from 0.1 to 1.9
- cand_ids: int32 [8, 2048], P('groups'), parts along dimension 0, may hold values from 0 to 255
- ranker: int32 [4], replicated, may hold values from 0 to 3, each once
- hist_blocks: int32 [8], P('groups'), parts along dimension 0, may hold values from 4 to 16, as said below
- cache_slot: int32 [8, 16], P('groups'), parts along dimension 0, may hold values from 0 to 63, as said below
Outputs:
- ranked: bfloat16 [16384, 1024], P(('groups', 'rank')), parts along dimension 0
There are 2 independent parts, one for each index of `groups`. A program takes and returns all parts, laid end to end along the dimension named above; an argument that names none is the same for every part. Nothing has to cross between parts.
Inputs may be any that keep to these rules, and one draw needn't show every extreme that they name: Block b of user u (b < 16) is held in slot cache_slot[u, b], which lies on device cache_slot[u, b] // 4 of the rank axis. Each slot holds exactly one pair (u, b); the 16 blocks of one user lie on 16 different devices. `ranker`: each ranking group scores exactly one user. User u's history is its blocks 0 to hist_blocks[u] - 1; its other blocks are unused. Some user has 16 blocks.
All inputs are finite; a program needn't handle non-finite values.
Results may differ from a plain program's by a relative error of at most 0.0054.
Values may be sent and summed in bfloat16 or wider, within the bound.
A program may use at most 128 MiB of HBM per device.

v0:
```python
import math

import jax
import jax.numpy as jnp
from jax import lax
from jax.sharding import PartitionSpec as P

norm_eps = 1e-05


def partner(shard, axis, bit):
    return lax.ppermute(shard, axis, [(i, i ^ 1 << bit) for i in range(lax.axis_size(axis))])


def attend_blocks(queries, stacked, head_dim, live_steps):
    score_scale = 1.0 / math.sqrt(head_dim)

    def step_fn(running, item):
        step_index, key_block = item

        def compute(total):
            key_part = key_block[:, :head_dim]
            value_part = key_block[:, head_dim:]
            scores = lax.dot_general(
                queries, key_part, (((1,), (1,)), ((), ())), preferred_element_type=jnp.float32
            )
            weights = jax.nn.silu(scores * score_scale).astype(jnp.bfloat16)
            return total + jnp.dot(weights, value_part, preferred_element_type=jnp.float32)

        def keep_same(total):
            return total

        return (lax.cond(step_index < live_steps, compute, keep_same, running), None)

    initial = jnp.zeros((queries.shape[0], head_dim), jnp.float32)
    step_ids = jnp.arange(stacked.shape[0], dtype=jnp.int32)
    attended, unused = lax.scan(step_fn, initial, (step_ids, stacked))
    return attended


def body(pool, kv_cache, w_qu, w_out, norm_gain, cand_ids, ranker, hist_blocks, cache_slot):
    devices = lax.axis_size("rank")
    my_index = lax.axis_index("rank")
    slots_here, head_count, block_len, pair_width = kv_cache.shape
    head_dim = pair_width // 2
    user_count, most_blocks = cache_slot.shape
    model_width = pool.shape[1]
    cand_count = cand_ids.shape[1]
    slice_width = model_width // head_count
    qu_cols = 2 * head_dim
    my_group = my_index // head_count
    my_head = my_index % head_count
    bit_count = head_count.bit_length() - 1
    share_rows = cand_count // head_count
    user_range = jnp.arange(user_count, dtype=jnp.int32)
    group_match = ranker[None, :] == user_range[:, None]
    user_of_group = jnp.sum(jnp.where(group_match, user_range[None, :], 0), axis=1)
    my_user = jnp.sum(jnp.where(user_range == my_group, user_of_group, 0))
    block_range = jnp.arange(most_blocks, dtype=jnp.int32)
    live_blocks = block_range[None, :] < hist_blocks[:, None]
    owner_table = cache_slot // slots_here
    held_here = live_blocks & (owner_table == my_index)
    held_slot = jnp.sum(jnp.where(held_here, cache_slot % slots_here, 0), axis=1)
    held_flag = jnp.any(held_here, axis=1)
    slot_of_group = jnp.sum(jnp.where(group_match, held_slot[None, :], 0), axis=1)
    flag_of_group = jnp.any(group_match & held_flag[None, :], axis=1)
    outgoing = jnp.take(kv_cache, slot_of_group, axis=0)
    outgoing = jnp.where(flag_of_group[:, None, None, None], outgoing, jnp.zeros_like(outgoing))
    outgoing = outgoing.reshape(devices, block_len, pair_width)
    incoming = lax.all_to_all(outgoing, "rank", split_axis=0, concat_axis=0, tiled=True)
    my_ids = lax.dynamic_index_in_dim(cand_ids, my_user, 0, keepdims=False)
    whole_pool = lax.all_gather(pool, "rank", axis=0, tiled=True)
    cand_rows = jnp.take(whole_pool, my_ids, axis=0)
    w_head = lax.dynamic_slice_in_dim(w_qu, my_head * qu_cols, qu_cols, 1)
    head_qu = jax.nn.silu(jnp.dot(cand_rows, w_head, preferred_element_type=jnp.float32)).astype(
        jnp.bfloat16
    )
    x_part = lax.dynamic_slice_in_dim(cand_rows, my_head * slice_width, slice_width, 1)
    queries = head_qu[:, :head_dim]
    gate_part = head_qu[:, head_dim:]
    step_sources = min(16, devices)
    stacked = incoming.reshape(devices // step_sources, step_sources * block_len, pair_width)
    live_steps = stacked.shape[0]
    attended = attend_blocks(queries, stacked, head_dim, live_steps)
    total_width = head_count * head_dim
    carried = jnp.concatenate(
        [attended, gate_part.astype(jnp.float32), x_part.astype(jnp.float32)], axis=1
    )
    state = carried.reshape(head_count, share_rows, 1, carried.shape[1])
    for bit_index in reversed(range(bit_count)):
        half_count = state.shape[0] // 2
        lower_half = state[:half_count]
        upper_half = state[half_count:]
        upper_side = my_head >> bit_index & 1 == 1
        keeping = jnp.where(upper_side, upper_half, lower_half)
        giving = jnp.where(upper_side, lower_half, upper_half)
        received = partner(giving, "rank", bit_index)
        state = jnp.where(
            upper_side,
            jnp.concatenate([received, keeping], axis=2),
            jnp.concatenate([keeping, received], axis=2),
        )
    reversal = [
        sum(((source >> bit & 1) << bit_count - 1 - bit for bit in range(bit_count)))
        for source in range(head_count)
    ]
    ordered = state[0][:, jnp.array(reversal, dtype=jnp.int32), :]
    att_rows = ordered[:, :, :head_dim].reshape(share_rows, total_width)
    gate_rows = ordered[:, :, head_dim:qu_cols].reshape(share_rows, total_width)
    x_rows = ordered[:, :, qu_cols:].reshape(share_rows, model_width)
    mean_value = jnp.mean(att_rows, axis=1, keepdims=True)
    variance = jnp.mean(att_rows * att_rows, axis=1, keepdims=True) - mean_value * mean_value
    hidden = (
        (att_rows - mean_value) * lax.rsqrt(variance + norm_eps) * norm_gain[None, :] * gate_rows
    ).astype(jnp.bfloat16)
    my_rows = x_rows + jnp.dot(hidden, w_out, preferred_element_type=jnp.float32)
    return my_rows.astype(jnp.bfloat16)


def solution(mesh):
    in_specs = (
        P(("groups", "rank"), None),
        P(("groups", "rank"), None, None, None),
        P(),
        P(),
        P(),
        P("groups", None),
        P(),
        P("groups"),
        P("groups", None),
    )
    out_specs = P(("groups", "rank"), None)
    return jax.shard_map(body, mesh=mesh, in_specs=in_specs, out_specs=out_specs, check_vma=False)
```

profile of v0, /device:TPU:0, one launch (start us, length us, event | category | flops | bytes accessed | tf_op | source)
XLA Modules:
  0.0 151.2 jit_solution(3385824127241586557)
XLA Ops:
  0.0 0.0 copy-start
  0.0 1.0 fusion.26
  1.0 0.8 fusion.16
  1.8 0.8 select_reduce_fusion
  2.7 0.1 broadcast_in_dim.84
  2.7 0.1 broadcast_in_dim.85
  2.8 0.8 fusion.18
  3.6 0.1 broadcast_in_dim.80
  3.7 0.1 broadcast_in_dim.81
  3.8 1.6 %gather_fusion.1 = bf16[4,4,64,256]{3,2,1,0:T(8,128)(2,1)S(1)} fusion(bf16[4,4,64,256]{3,2,1,0:T(8,128)(2,1)} %param.11, s32[1024]{0:T(1024)S(1)} %pad_clamp_fusion.1), kind=kCustom, calls=%fused_computation.1 | custom fusion | bytes 1048592 | tf_op jit(solution)/shard_map/jit(_take)/gather | solution.py:67
  5.4 1.0 fusion.6
  6.4 7.4 %all-to-all-start = ((bf16[16,64,256]{2,1,0:T(8,128)(2,1)}), bf16[16,64,256]{2,1,0:T(8,128)(2,1)}, u32[]{:S(2)}, u32[]{:S(2)}) async-start(bf16[16,64,256]{2,1,0:T(8,128)(2,1)} %fusion.6), calls=%async_computation | async-start | bytes 1048576 | tf_op jit(solution)/shard_map/all_to_all | solution.py:70
  13.8 0.6 fusion.22
  16.4 0.8 compare_select_fusion
  17.2 23.5 %all_gather.3 = bf16[256,1024]{1,0:T(8,128)(2,1)S(1)} all-gather(bf16[16,1024]{1,0:T(8,128)(2,1)} %param.10), channel_id=1, replica_groups=mesh['groups'=2,'rank'=16] {'rank'}, dimensions={0}, use_global_device_ids=true | all-gather | bytes 557056 | tf_op jit(solution)/shard_map/all_gather | solution.py:72
  40.7 9.7 %gather_fusion = bf16[2048,1024]{1,0:T(8,128)(2,1)} fusion(bf16[256,1024]{1,0:T(8,128)(2,1)S(1)} %all_gather.3, s32[2048]{0:T(1024)S(1)} %broadcast_clamp_fusion), kind=kCustom, calls=%fused_computation | custom fusion | bytes 8396800 | tf_op jit(solution)/shard_map/jit(_take)/gather | solution.py:73
  50.3 3.8 %broadcast_select_fusion = bf16[2048,1024]{1,0:T(8,128)(2,1)} fusion(bf16[2048,1024]{1,0:T(8,128)(2,1)} %gather_fusion, pred[2048]{0:T(1024)(128)(4,1)S(1)} %compare_and_fusion), kind=kLoop, calls=%fused_computation.7 | loop fusion | flops 2097152 | bytes 8390656 | tf_op jit(solution)/shard_map/jit(_take)/select_n | solution.py:73
  54.1 0.0 copy-done
  54.1 4.8 %multiply_convert_fusion.1 = bf16[2048,256]{0,1:T(8,128)(2,1)} fusion(bf16[2048,1024]{1,0:T(8,128)(2,1)} %broadcast_select_fusion, bf16[1024,1024]{1,0:T(8,128)(2,1)S(1)} %copy-done, s32[]{:T(128)S(6)} %select_n.171), kind=kOutput, calls=%fused_computation.11 | convolution fusion | flops 1076363264 | bytes 5767172 | tf_op jit(solution)/shard_map/dot_general | solution.py:75
  58.9 1.1 slice_convert_fusion
  60.0 1.3 copy.32
  61.4 2.7 %dynamic-slice_convert_fusion = f32[2048,256]{1,0:T(8,128)} fusion(bf16[2048,1024]{1,0:T(8,128)(2,1)} %broadcast_select_fusion, s32[]{:T(128)S(6)} %select_n.171), kind=kLoop, calls=%fused_computation.22 | loop fusion | flops 524288 | bytes 3145732 | tf_op jit(solution)/shard_map/convert_element_type | solution.py:87
  64.1 0.0 all-to-all-done
  64.1 4.8 %fusion = f32[2048,128]{1,0:T(8,128)} fusion(bf16[2048,256]{0,1:T(8,128)(2,1)} %multiply_convert_fusion.1, bf16[1024,256]{1,0:T(8,128)(2,1)} %bitcast.6), kind=kOutput, calls=%fused_computation.15 | convolution fusion | flops 1086324736 | bytes 2097152 | tf_op jit(solution)/shard_map/while/body/eval_jaxpr/cond/branch_1_fun/dot_general | solution.py:28
  68.9 0.0 copy-done.4
  68.9 2.3 %pad_maximum_fusion = f32[2048,512]{1,0:T(8,128)S(1)} fusion(f32[2048,256]{1,0:T(8,128)} %dynamic-slice_convert_fusion, f32[2048,128]{1,0:T(8,128)S(1)} %copy-done.4, f32[2048,128]{1,0:T(8,128)} %fusion), kind=kLoop, calls=%fused_computation.4 | loop fusion | flops 2097152 | bytes 8388608 | tf_op jit(solution)/shard_map/concatenate | solution.py:86
  71.2 2.4 %slice_select_fusion.2 = (f32[1024,512]{1,0:T(8,128)}, f32[1024,512]{1,0:T(8,128)}) fusion(f32[2048,512]{1,0:T(8,128)S(1)} %pad_maximum_fusion, pred[]{:T(512)S(6)} %eq.36), kind=kLoop, calls=%fused_computation.14 | loop fusion | flops 1048576 | bytes 8388609 | tf_op jit(solution)/shard_map/jit(_where)/select_n | solution.py:96
  73.6 1.6 %collective-permute-start = (f32[2,512,1,512]{3,1,2,0:T(8,128)}, f32[2,512,1,512]{3,1,2,0:T(8,128)}, u32[]{:S(2)}, u32[]{:S(2)}) collective-permute-start(f32[2,512,1,512]{3,1,2,0:T(8,128)} %bitcast.8), channel_id=1, source_target_pairs={{0,2},{1,3},{2,0},{3,1},{4,6},{5,7},{6,4},{7,5},{8,10},{9,11},{10,... | collective-permute-start | bytes 6291464 | tf_op jit(solution)/shard_map/ppermute | solution.py:12
  75.2 46.6 %collective-permute-done = f32[2,512,1,512]{3,1,2,0:T(8,128)} collective-permute-done((f32[2,512,1,512]{3,1,2,0:T(8,128)}, f32[2,512,1,512]{3,1,2,0:T(8,128)}, u32[]{:S(2)}, u32[]{:S(2)}) %collective-permute-start) | collective-permute-done | bytes 2097184 | tf_op jit(solution)/shard_map/ppermute | solution.py:12
  121.8 4.5 %maximum_select_fusion = f32[2,512,2,512]{3,1,2,0:T(8,128)S(1)} fusion(f32[2,512,1,512]{3,1,2,0:T(8,128)} %bitcast.45, f32[2,512,1,512]{3,1,2,0:T(8,128)} %collective-permute-done, pred[]{:T(512)S(6)} %eq.36), kind=kLoop, calls=%fused_computation.5 | loop fusion | flops 3145728 | bytes 8388609 | tf_op jit(solution)/shard_map/jit(_where)/select_n | solution.py:98
  126.3 0.0 copy-start.7
  126.4 0.5 slice_select_fusion
  126.9 0.1 collective-permute-start.1
  126.9 0.1 copy-done.7
  127.0 4.1 %collective-permute-done.1 = f32[1,512,2,512]{3,1,2,0:T(8,128)S(1)} collective-permute-done((f32[1,512,2,512]{3,1,2,0:T(8,128)S(1)}, f32[1,512,2,512]{3,1,2,0:T(8,128)S(1)}, u32[]{:S(2)}, u32[]{:S(2)}) %collective-permute-start.1) | collective-permute-done | bytes 2097184 | tf_op jit(solution)/shard_map/ppermute | solution.py:12
  131.1 2.5 %maximum_select_fusion.1 = f32[512,4,512]{2,0,1:T(8,128)} fusion(f32[512,2,512]{2,0,1:T(8,128)S(1)} %get-tuple-element.37, f32[512,2,512]{2,0,1:T(8,128)S(1)} %bitcast.46, pred[]{:T(512)S(6)} %eq.35), kind=kLoop, calls=%fused_computation.6 | loop fusion | flops 3145728 | bytes 8388609 | tf_op jit(solution)/shard_map/jit(_where)/select_n | solution.py:98
  133.5 5.0 %gather_fusion.2 = f32[4,512,512]{2,1,0:T(8,128)} fusion(f32[512,4,512]{2,0,1:T(8,128)} %maximum_select_fusion.1, s32[1024]{0:T(1024)S(1)} %pad_clamp_fusion), kind=kCustom, calls=%fused_computation.2 | custom fusion | bytes 8388624 | tf_op jit(solution)/shard_map/gather | solution.py:107
  138.5 2.8 %slice_reduce_fusion = (f32[512]{0:T(512)S(1)}, f32[512]{0:T(512)S(1)}, f32[512,4,128]{2,0,1:T(8,128)}, f32[512,4,128]{2,0,1:T(8,128)S(1)}) fusion(f32[512,4,512]{2,0,1:T(8,128)} %bitcast.42), kind=kLoop, calls=%fused_computation.67 | loop fusion | flops 785408 | bytes 4198400 | tf_op jit(solution)/shard_map/reduce_sum | solution.py:111
  141.3 0.2 copy-done.1
  141.6 1.6 %slice_bitcast_fusion = f32[4,64,8,256]{3,2,1,0:T(8,128)} fusion(f32[512,4,512]{2,0,1:T(8,128)S(1)} %bitcast.43), kind=kLoop, calls=%fused_computation.8 | loop fusion | bytes 4194304
  143.1 2.6 %copy.37 = f32[512,4,128]{0,2,1:T(8,128)} copy(f32[512,4,128]{2,0,1:T(8,128)} %get-tuple-element.34) | data formatting | bytes 2097152 | tf_op jit(solution)/shard_map/slice | solution.py:108
  145.7 1.3 copy.38
  147.0 2.0 %copy.40 = f32[4,64,8,256]{3,2,0,1:T(8,128)S(1)} copy(f32[4,64,8,256]{3,2,1,0:T(8,128)} %slice_bitcast_fusion) | data formatting | bytes 4194304 | tf_op jit(solution)/shard_map/reshape | solution.py:110
  149.0 0.0 copy-done.6
  149.0 0.1 copy-done.3
  149.2 0.2 fusion.1
  149.4 0.1 copy-done.5
  149.5 1.7 %add_convert_fusion = bf16[512,1024]{1,0:T(8,128)(2,1)} fusion(f32[512,1024]{1,0:T(8,128)S(1)} %bitcast.44, bf16[512,512]{0,1:T(8,128)(2,1)S(1)} %fusion.1, bf16[512,1024]{1,0:T(8,128)(2,1)S(1)} %copy-done.5), kind=kOutput, calls=%fused_computation.9 | convolution fusion | flops 537919488 | bytes 4718592 | tf_op jit(solution)/shard_map/dot_general | solution.py:116
  (14 shorter events, 0.1 us)
Async XLA Ops:
  0.0 54.1 %copy-start = (bf16[1024,1024]{1,0:T(8,128)(2,1)S(1)}, bf16[1024,1024]{1,0:T(8,128)(2,1)}, u32[]{:S(2)}) copy-start(bf16[1024,1024]{1,0:T(8,128)(2,1)} %param.12) | copy-start | bytes 6291460
  6.4 57.7 %all-to-all-start = ((bf16[16,64,256]{2,1,0:T(8,128)(2,1)}), bf16[16,64,256]{2,1,0:T(8,128)(2,1)}, u32[]{:S(2)}, u32[]{:S(2)}) async-start(bf16[16,64,256]{2,1,0:T(8,128)(2,1)} %fusion.6), calls=%async_computation | async-start | bytes 1048576 | tf_op jit(solution)/shard_map/all_to_all | solution.py:70
  64.1 4.8 %copy-start.4 = (f32[2048,128]{1,0:T(8,128)S(1)}, f32[2048,128]{1,0:T(8,128)}, u32[]{:S(2)}) copy-start(f32[2048,128]{1,0:T(8,128)} %copy.32) | copy-start | bytes 3145732
  73.6 48.2 %collective-permute-start = (f32[2,512,1,512]{3,1,2,0:T(8,128)}, f32[2,512,1,512]{3,1,2,0:T(8,128)}, u32[]{:S(2)}, u32[]{:S(2)}) collective-permute-start(f32[2,512,1,512]{3,1,2,0:T(8,128)} %bitcast.8), channel_id=1, source_target_pairs={{0,2},{1,3},{2,0},{3,1},{4,6},{5,7},{6,4},{7,5},{8,10},{9,11},{10,... | collective-permute-start | bytes 6291464 | tf_op jit(solution)/shard_map/ppermute | solution.py:12
  126.3 0.7 copy-start.7
  126.9 4.2 %collective-permute-start.1 = (f32[1,512,2,512]{3,1,2,0:T(8,128)S(1)}, f32[1,512,2,512]{3,1,2,0:T(8,128)S(1)}, u32[]{:S(2)}, u32[]{:S(2)}) collective-permute-start(f32[1,512,2,512]{3,1,2,0:T(8,128)S(1)} %get-tuple-element.36), channel_id=1, source_target_pairs={{0,1},{1,0},{2,3},{3,2},{4,5},{5,4},{6,7},{7,6},{8,9},{9,8},{10,11... | collective-permute-start | bytes 6291464 | tf_op jit(solution)/shard_map/ppermute | solution.py:12
  138.5 3.0 %copy-start.1 = (f32[4,512,512]{2,1,0:T(8,128)S(1)}, f32[4,512,512]{2,1,0:T(8,128)}, u32[]{:S(2)}) copy-start(f32[4,512,512]{2,1,0:T(8,128)} %gather_fusion.2) | copy-start | bytes 12582916
  143.1 5.9 %copy-start.6 = (f32[512]{0:T(512)S(1)}, f32[512]{0:T(512)}, u32[]{:S(2)}) copy-start(f32[512]{0:T(512)} %param.14) | copy-start | bytes 6148
  147.0 2.0 %copy-start.2 = (f32[512,4,128]{0,2,1:T(8,128)S(1)}, f32[512,4,128]{0,2,1:T(8,128)}, u32[]{:S(2)}) copy-start(f32[512,4,128]{0,2,1:T(8,128)} %copy.37) | copy-start | bytes 3145732
  147.0 2.2 %copy-start.3 = (f32[512,4,128]{0,2,1:T(8,128)S(1)}, f32[512,4,128]{0,2,1:T(8,128)}, u32[]{:S(2)}) copy-start(f32[512,4,128]{0,2,1:T(8,128)} %copy.38) | copy-start | bytes 3145732
  147.0 2.5 %copy-start.5 = (bf16[512,1024]{1,0:T(8,128)(2,1)S(1)}, bf16[512,1024]{1,0:T(8,128)(2,1)}, u32[]{:S(2)}) copy-start(bf16[512,1024]{1,0:T(8,128)(2,1)} %param.13) | copy-start | bytes 3145732
where the time goes:
time: 152 us; the launch traced here: 151 us
  waiting for transfers between devices  50.7 us (33%)
  other arithmetic  28.6 us (19%)
  local copies, waits for them, and re-layouts  25.9 us (17%)
  blocking collectives  23.5 us (15%)
  matrix products  11.3 us (7%)
  starting transfers between devices  9.08 us (6%)
  between operations  2.11 us (1%)
    ppermute x2, waiting for transfers between devices, partner(): lax.ppermute(shard, axis, [(i, i ^ 1 << bit) for i in range(lax.axis_size...  50.7 us
    all_gather x1, blocking collectives, body(): whole_pool = lax.all_gather(pool, 'rank', axis=0, tiled=True)  23.5 us
    gather x1, local copies, waits for them, and re-layouts, body(): cand_rows = jnp.take(whole_pool, my_ids, axis=0)  9.66 us
    all_to_all x1, starting transfers between devices, body(): lax.all_to_all(outgoing, 'rank', split_axis=0, concat_axis=0, tiled=True)  7.41 us
    select_n x2, other arithmetic, body(): jnp.where(upper_side, jnp.concatenate([received, keeping], axis=2), jnp.c...  6.96 us
    gather x1, local copies, waits for them, and re-layouts, body(): ordered = state[0][:, jnp.array(reversal, dtype=jnp.int32), :]  4.97 us
    dot_general x1, matrix products, compute(): jnp.dot(weights, value_part, preferred_element_type=jnp.float32)  4.83 us
    dot_general x1, matrix products, body(): jnp.dot(cand_rows, w_head, preferred_element_type=jnp.float32)  4.77 us
  transfers between devices with their start and end apart: 3, of which 2 were waited for; matrix products, arithmetic and copies ran while one was open for 16% of the time, Pallas kernels for 0%

commit v1 on v0

--- a/solution.py
+++ b/solution.py
@@ -1,11 +1,15 @@
+import functools
 import math
 
 import jax
 import jax.numpy as jnp
 from jax import lax
+from jax.experimental import pallas as pl
+from jax.experimental.pallas import tpu as pltpu
 from jax.sharding import PartitionSpec as P
 
 norm_eps = 1e-05
+MESH = pl.DeviceIdType.MESH
 
 
 def partner(shard, axis, bit):
@@ -38,7 +42,7 @@
     return attended
 
 
-def body(pool, kv_cache, w_qu, w_out, norm_gain, cand_ids, ranker, hist_blocks, cache_slot):
+def candidate_body(pool, kv_cache, w_qu, w_out, norm_gain, cand_ids, ranker, hist_blocks, cache_slot):
     devices = lax.axis_size("rank")
     my_index = lax.axis_index("rank")
     slots_here, head_count, block_len, pair_width = kv_cache.shape
@@ -117,6 +121,335 @@
     return my_rows.astype(jnp.bfloat16)
 
 
+def silu(x):
+    half = x * 0.5
+    return half + half * jnp.tanh(half)
+
+
+def item_kernel(
+    devices,
+    slots_ref,
+    ranker_ref,
+    blocks_ref,
+    cand_ref,
+    gain_ref,
+    pool_ref,
+    kv_ref,
+    wqu_hbm,
+    wout_hbm,
+    out_ref,
+    items,
+    picked,
+    history,
+    wqu,
+    wout,
+    head_qu,
+    partial,
+    core_in,
+    chip_sum,
+    chip_in,
+    hidden,
+    table,
+    onehot,
+    load_sem,
+    pool_send,
+    pool_recv,
+    kv_send,
+    kv_recv,
+    core_send,
+    core_recv,
+    chip_send,
+    chip_recv,
+    hid_send,
+    hid_recv,
+):
+    me = lax.axis_index("rank")
+    slots_here, head_count, block_len, pair_width = kv_ref.shape
+    head_dim = pair_width // 2
+    user_count, most_blocks = slots_ref.shape
+    rows_here, model_width = pool_ref.shape
+    item_count = devices * rows_here
+    half_items = item_count // 2
+    share_rows = out_ref.shape[0]
+    team = devices // user_count
+    bits = devices.bit_length() - 1
+    score_scale = 1.0 / math.sqrt(head_dim)
+
+    def bit_of(j):
+        return (me // (1 << j)) % 2
+
+    def flipped(mask):
+        other = me
+        for j in range(bits):
+            if mask >> j & 1:
+                other = other + (1 << j) * (1 - 2 * bit_of(j))
+        return other
+
+    my_group = me // team
+    share = me % team
+    core = bit_of(0)
+
+    load_qu = pltpu.make_async_copy(wqu_hbm, wqu, load_sem.at[0])
+    load_out = pltpu.make_async_copy(wout_hbm, wout, load_sem.at[1])
+    load_qu.start()
+    load_out.start()
+
+    barrier = pltpu.get_barrier_semaphore()
+    masks = [1, 2] + [team * d for d in range(1, user_count)]
+    for mask in masks:
+        pl.semaphore_signal(
+            barrier, inc=1, device_id={"rank": flipped(mask)}, device_id_type=MESH
+        )
+
+    place = 0
+    for j in range(bits):
+        place = place + bit_of(j) * (1 << (bits - 1 - j))
+    items[place] = pool_ref[...]
+    held, alive = [], []
+    for u in range(user_count):
+        slot, live = jnp.int32(0), jnp.int32(0)
+        for b in range(most_blocks):
+            entry = slots_ref[u, b]
+            mine = lax.div(entry, slots_here) == me
+            slot = jnp.where(mine, lax.rem(entry, slots_here), slot)
+            live = jnp.where(mine & (b < blocks_ref[u]), 1, live)
+        held.append(slot)
+        alive.append(live)
+    for g in range(user_count):
+        slot, live = jnp.int32(0), jnp.int32(0)
+        for u in range(user_count):
+            here = ranker_ref[u] == g
+            slot = jnp.where(here, held[u], slot)
+            live = jnp.where(here, alive[u], live)
+        block = kv_ref[slot]
+        picked[g] = jnp.where(live == 1, block, jnp.zeros_like(block))
+
+    pl.semaphore_wait(barrier, len(masks))
+
+    def pool_step(j):
+        span = 1 << (bits - 1 - j)
+        part = items.at[pl.ds((place // span) * span, span)]
+        return pltpu.make_async_remote_copy(
+            src_ref=part,
+            dst_ref=part,
+            send_sem=pool_send.at[j],
+            recv_sem=pool_recv.at[j],
+            device_id={"rank": flipped(1 << j)},
+            device_id_type=MESH,
+        )
+
+    def kv_copy(h, d):
+        other = flipped(team * d)
+        return pltpu.make_async_remote_copy(
+            src_ref=picked.at[other // team, h],
+            dst_ref=history.at[h, d],
+            send_sem=kv_send.at[h, d - 1],
+            recv_sem=kv_recv.at[h, d - 1],
+            device_id={"rank": other},
+            device_id_type=MESH,
+        )
+
+    pool_step(bits - 1).start()
+    kv_copies = {}
+    for h in range(head_count):
+        for d in reversed(range(1, user_count)):
+            kv_copies[h, d] = kv_copy(h, d)
+            kv_copies[h, d].start()
+
+    for h in range(head_count):
+        history[h, 0] = picked[my_group, h]
+
+    first = pl.multiple_of(share * share_rows, share_rows)
+    ids = jnp.zeros((1, share_rows), jnp.int32)
+    for u in range(user_count):
+        ids = jnp.where(ranker_ref[u] == my_group, cand_ref[pl.ds(u, 1), pl.ds(first, share_rows)], ids)
+    row = lax.broadcasted_iota(jnp.int32, (item_count, share_rows), 0)
+    block_at = row // rows_here
+    rank_at = jnp.zeros_like(row)
+    for j in range(bits):
+        rank_at = rank_at + ((block_at >> j) & 1) * (1 << (bits - 1 - j))
+    item_at = rank_at * rows_here + row % rows_here
+    hits = (item_at == ids).astype(jnp.float32)
+    onehot[...] = hits.T.astype(jnp.bfloat16)
+
+    for j in reversed(range(bits)):
+        step = pool_step(j)
+        if j < bits - 1:
+            step.start()
+        step.wait()
+
+    load_qu.wait()
+    all_items = items[...].reshape(item_count, model_width)
+    for h in range(head_count):
+        qu = jnp.dot(
+            all_items,
+            wqu[:, h * pair_width : (h + 1) * pair_width],
+            preferred_element_type=jnp.float32,
+        )
+        head_qu[h] = silu(qu).astype(jnp.bfloat16)
+
+    mine_at = pl.multiple_of(core * half_items, half_items)
+    other_at = pl.multiple_of((1 - core) * half_items, half_items)
+
+    def core_copy(h):
+        return pltpu.make_async_remote_copy(
+            src_ref=partial.at[h, pl.ds(other_at, half_items)],
+            dst_ref=core_in.at[h],
+            send_sem=core_send.at[h],
+            recv_sem=core_recv.at[h],
+            device_id={"rank": flipped(1)},
+            device_id_type=MESH,
+        )
+
+    def chip_copy(h):
+        return pltpu.make_async_remote_copy(
+            src_ref=chip_sum.at[h],
+            dst_ref=chip_in.at[h],
+            send_sem=chip_send.at[h],
+            recv_sem=chip_recv.at[h],
+            device_id={"rank": flipped(2)},
+            device_id_type=MESH,
+        )
+
+    def to_chip(h):
+        core_copy(h).wait()
+        chip_sum[h] = partial[h, pl.ds(mine_at, half_items)] + core_in[h]
+        chip_copy(h).start()
+
+    for h in range(head_count):
+        for d in range(1, user_count):
+            kv_copies[h, d].wait()
+        pairs = history[h].reshape(user_count * block_len, pair_width)
+        scores = lax.dot_general(
+            head_qu[h, :, :head_dim],
+            pairs[:, :head_dim],
+            (((1,), (1,)), ((), ())),
+            preferred_element_type=jnp.float32,
+        )
+        weights = silu(scores * score_scale).astype(jnp.bfloat16)
+        partial[h] = jnp.dot(weights, pairs[:, head_dim:], preferred_element_type=jnp.float32)
+        core_copy(h).start()
+        if h > 0:
+            to_chip(h - 1)
+    to_chip(head_count - 1)
+
+    attended = []
+    for h in range(head_count):
+        chip_copy(h).wait()
+        attended.append(chip_sum[h] + chip_in[h])
+    width = head_count * head_dim
+    mean = sum(jnp.sum(a, axis=1, keepdims=True) for a in attended) / width
+    square = sum(jnp.sum(a * a, axis=1, keepdims=True) for a in attended) / width
+    scale = lax.rsqrt(square - mean * mean + norm_eps)
+    for h in range(head_count):
+        columns = slice(h * head_dim, (h + 1) * head_dim)
+        gate = head_qu[h, pl.ds(mine_at, half_items), head_dim:].astype(jnp.float32)
+        normed = (attended[h] - mean) * scale * gain_ref[:, columns] * gate
+        hidden[pl.ds(mine_at, half_items), columns] = normed.astype(jnp.bfloat16)
+
+    own_half = hidden.at[pl.ds(mine_at, half_items)]
+    swap = pltpu.make_async_remote_copy(
+        src_ref=own_half,
+        dst_ref=own_half,
+        send_sem=hid_send,
+        recv_sem=hid_recv,
+        device_id={"rank": flipped(1)},
+        device_id_type=MESH,
+    )
+    swap.start()
+    load_out.wait()
+
+    half_blocks = devices // 2
+
+    def project(at, block_from):
+        base = items[pl.ds(block_from, half_blocks)].reshape(half_items, model_width)
+        mixed = base.astype(jnp.float32) + jnp.dot(
+            hidden[pl.ds(at, half_items)], wout[...], preferred_element_type=jnp.float32
+        )
+        table[pl.ds(at, half_items)] = mixed.astype(jnp.bfloat16)
+
+    project(mine_at, core * half_blocks)
+    swap.wait()
+    project(other_at, (1 - core) * half_blocks)
+    out_ref[...] = jnp.dot(
+        onehot[...], table[...], preferred_element_type=jnp.float32
+    ).astype(jnp.bfloat16)
+
+
+def item_body(pool, kv_cache, w_qu, w_out, norm_gain, cand_ids, ranker, hist_blocks, cache_slot):
+    devices = lax.axis_size("rank")
+    slots_here, head_count, block_len, pair_width = kv_cache.shape
+    head_dim = pair_width // 2
+    user_count = cache_slot.shape[0]
+    rows_here, model_width = pool.shape
+    item_count = devices * rows_here
+    half_items = item_count // 2
+    share_rows = cand_ids.shape[1] * user_count // devices
+    width = head_count * head_dim
+    bits = devices.bit_length() - 1
+    smem = pl.BlockSpec(memory_space=pltpu.SMEM)
+    vmem = pl.BlockSpec(memory_space=pltpu.VMEM)
+    hbm = pl.BlockSpec(memory_space=pl.ANY)
+    dma = pltpu.SemaphoreType.DMA
+    narrow, wide = jnp.bfloat16, jnp.float32
+    return pl.pallas_call(
+        functools.partial(item_kernel, devices),
+        out_shape=jax.ShapeDtypeStruct((share_rows, model_width), narrow),
+        in_specs=[smem, smem, smem, vmem, vmem, vmem, vmem, hbm, hbm],
+        out_specs=vmem,
+        scratch_shapes=[
+            pltpu.VMEM((devices, rows_here, model_width), narrow),
+            pltpu.VMEM((user_count, head_count, block_len, pair_width), narrow),
+            pltpu.VMEM((head_count, user_count, block_len, pair_width), narrow),
+            pltpu.VMEM(w_qu.shape, narrow),
+            pltpu.VMEM(w_out.shape, narrow),
+            pltpu.VMEM((head_count, item_count, pair_width), narrow),
+            pltpu.VMEM((head_count, item_count, head_dim), wide),
+            pltpu.VMEM((head_count, half_items, head_dim), wide),
+            pltpu.VMEM((head_count, half_items, head_dim), wide),
+            pltpu.VMEM((head_count, half_items, head_dim), wide),
+            pltpu.VMEM((item_count, width), narrow),
+            pltpu.VMEM((item_count, model_width), narrow),
+            pltpu.VMEM((share_rows, item_count), narrow),
+            dma((2,)),
+            dma((bits,)),
+            dma((bits,)),
+            dma((head_count, user_count - 1)),
+            dma((head_count, user_count - 1)),
+            dma((head_count,)),
+            dma((head_count,)),
+            dma((head_count,)),
+            dma((head_count,)),
+            dma,
+            dma,
+        ],
+        compiler_params=pltpu.CompilerParams(
+            collective_id=0, has_side_effects=True, vmem_limit_bytes=40 * 1024 * 1024
+        ),
+    )(
+        cache_slot,
+        ranker,
+        hist_blocks,
+        cand_ids,
+        norm_gain.reshape(1, width),
+        pool,
+        kv_cache,
+        w_qu,
+        w_out,
+    )
+
+
+def body(pool, kv_cache, w_qu, w_out, norm_gain, cand_ids, ranker, hist_blocks, cache_slot):
+    devices = lax.axis_size("rank")
+    user_count = cache_slot.shape[0]
+    items_fit = pool.shape[0] * devices * devices <= cand_ids.shape[1] * user_count
+    in_fours = devices == 4 * user_count and devices & (devices - 1) == 0
+    chosen = item_body if items_fit and in_fours and pool.shape[0] % 16 == 0 else candidate_body
+    return chosen(
+        pool, kv_cache, w_qu, w_out, norm_gain, cand_ids, ranker, hist_blocks, cache_slot
+    )
+
+
 def solution(mesh):
     in_specs = (
         P(("groups", "rank"), None),

time: 152 us -> 43.4 us (0.29)
  waiting for transfers between devices: 50.7 us -> 0 us
  Pallas kernels: 0 us -> 34 us
  other arithmetic: 28.6 us -> 0 us
  blocking collectives: 23.5 us -> 0 us
  local copies, waits for them, and re-layouts: 25.9 us -> 9.01 us
  matrix products: 11.3 us -> 0 us
  starting transfers between devices: 9.08 us -> 0 us
  between operations: 2.11 us -> 0.02 us
    ppermute x2 -> x0, waiting for transfers between devices: 50.7 us -> none  [partner(): lax.ppermute(shard, axis, [(i, i ^ 1 << bit) for i in range(lax.axis_size...]
    pallas_call x0 -> x1, Pallas kernels: none -> 34 us  [item_body(): pl.pallas_call(functools.partial(item_kernel, devices), out_shape=jax.Sha...]
    all_gather x1 -> x0, blocking collectives: 23.5 us -> none  [body(): whole_pool = lax.all_gather(pool, 'rank', axis=0, tiled=True)]
    gather x3 -> x0, local copies, waits for them, and re-layouts: 16.3 us -> none  [the longest x1 9.66 us: body(): cand_rows = jnp.take(whole_pool, my_ids, axis=0)]
    select_n x8 -> x0, other arithmetic: 15.4 us -> none  [the longest x2 6.96 us: body(): jnp.where(upper_side, jnp.concatenate([received, keeping], axis=2), jnp.c...]
    dot_general x3 -> x0, matrix products: 11.3 us -> none  [the longest x1 4.83 us: compute(): jnp.dot(weights, value_part, preferred_element_type=jnp.float32)]
    all_to_all x1 -> x0, starting transfers between devices: 7.41 us -> none  [body(): lax.all_to_all(outgoing, 'rank', split_axis=0, concat_axis=0, tiled=True)]
    unnamed x17 -> x19, local copies, waits for them, and re-layouts: 2.16 us -> 9.01 us
  transfers between devices with their start and end apart: 3 -> 0, of which waited for: 2 -> 0; matrix products, arithmetic and copies ran while one was open for 16% -> 0% of each run, Pallas kernels for 0% -> 0%
where the time goes in v1:
time: 43.4 us; the launch traced here: 43 us
  Pallas kernels  34 us (78%)
  local copies, waits for them, and re-layouts  9.01 us (21%)
    pallas_call x1, Pallas kernels, item_body(): pl.pallas_call(functools.partial(item_kernel, devices), out_shape=jax.Sha...  34 us
    unnamed x19, local copies, waits for them, and re-layouts  9.01 us

profile of v1, /device:TPU:0, one launch (start us, length us, event | category | flops | bytes accessed | tf_op | source)
XLA Modules:
  0.0 43.0 jit_solution(4798115688825855766)
XLA Ops:
  0.0 0.0 copy-start
  0.0 1.6 %copy-done = bf16[1024,1024]{1,0:T(8,128)(2,1)S(1)} copy-done((bf16[1024,1024]{1,0:T(8,128)(2,1)S(1)}, bf16[1024,1024]{1,0:T(8,128)(2,1)}, u32[]{:S(2)}) %copy-start) | copy-done | bytes 2097176
  1.6 0.0 copy-start.1
  1.6 1.2 %copy-done.1 = bf16[512,1024]{1,0:T(8,128)(2,1)S(1)} copy-done((bf16[512,1024]{1,0:T(8,128)(2,1)S(1)}, bf16[512,1024]{1,0:T(8,128)(2,1)}, u32[]{:S(2)}) %copy-start.1) | copy-done | bytes 1048600
  2.8 0.0 copy-start.2
  2.8 1.0 %copy-done.2 = bf16[4,4,64,256]{3,2,1,0:T(8,128)(2,1)S(1)} copy-done((bf16[4,4,64,256]{3,2,1,0:T(8,128)(2,1)S(1)}, bf16[4,4,64,256]{3,2,1,0:T(8,128)(2,1)}, u32[]{:S(2)}) %copy-start.2) | copy-done | bytes 524312
  3.9 0.0 copy-start.3
  3.9 0.8 %copy-done.3 = s32[4,2048]{1,0:T(4,128)S(1)} copy-done((s32[4,2048]{1,0:T(4,128)S(1)}, s32[4,2048]{1,0:T(4,128)}, u32[]{:S(2)}) %copy-start.3) | copy-done | bytes 32792
  4.6 0.0 copy-start.4
  4.6 0.8 %copy-done.4 = bf16[16,1024]{1,0:T(8,128)(2,1)S(1)} copy-done((bf16[16,1024]{1,0:T(8,128)(2,1)S(1)}, bf16[16,1024]{1,0:T(8,128)(2,1)}, u32[]{:S(2)}) %copy-start.4) | copy-done | bytes 32792
  5.4 0.0 copy-start.5
  5.4 0.7 %copy-done.5 = s32[4,16]{1,0:T(4,128)S(1)} copy-done((s32[4,16]{1,0:T(4,128)S(1)}, s32[4,16]{1,0:T(4,128)}, u32[]{:S(2)}) %copy-start.5) | copy-done | bytes 280
  6.1 0.0 copy-start.6
  6.1 0.7 %copy-done.6 = f32[512]{0:T(512)S(1)} copy-done((f32[512]{0:T(512)S(1)}, f32[512]{0:T(512)}, u32[]{:S(2)}) %copy-start.6) | copy-done | bytes 2072
  6.7 0.0 copy-start.7
  6.7 0.7 %copy-done.7 = s32[4]{0:T(128)S(1)} copy-done((s32[4]{0:T(128)S(1)}, s32[4]{0:T(128)}, u32[]{:S(2)}) %copy-start.7) | copy-done | bytes 40
  7.4 0.0 copy-start.8
  7.4 0.7 %copy-done.8 = s32[4]{0:T(128)S(1)} copy-done((s32[4]{0:T(128)S(1)}, s32[4]{0:T(128)}, u32[]{:S(2)}) %copy-start.8) | copy-done | bytes 40
  8.1 34.0 %shard_map.91 = bf16[512,1024]{1,0:T(8,128)(2,1)S(1)} custom-call(s32[4,16]{1,0:T(4,128)S(1)} %copy-done.5, s32[4]{0:T(128)S(1)} %copy-done.7, s32[4]{0:T(128)S(1)} %copy-done.8, s32[4,2048]{1,0:T(4,128)S(1)} %copy-done.3, f32[1,512]{1,0:T(1,128)S(1)} %bitcast.1, bf16[16,1024]{1,0:T(8,128)(2,1)S(1)} %copy-done.4, bf16[4,4,64,256]{3,2,1,0:T(8,128)(2,1)S(1)} %copy-done.2, ...), custom_call_target="tpu_custom_call" | custom-call | tf_op jit(solution)/shard_map/pallas_call | solution.py:395
  42.0 1.0 %copy.11 = bf16[512,1024]{1,0:T(8,128)(2,1)} copy(bf16[512,1024]{1,0:T(8,128)(2,1)S(1)} %shard_map.91) | data formatting | bytes 2097152
Async XLA Ops:
  0.0 1.6 %copy-start = (bf16[1024,1024]{1,0:T(8,128)(2,1)S(1)}, bf16[1024,1024]{1,0:T(8,128)(2,1)}, u32[]{:S(2)}) copy-start(bf16[1024,1024]{1,0:T(8,128)(2,1)} %wqu_hbm.1) | copy-start | bytes 6291460
  1.6 1.2 %copy-start.1 = (bf16[512,1024]{1,0:T(8,128)(2,1)S(1)}, bf16[512,1024]{1,0:T(8,128)(2,1)}, u32[]{:S(2)}) copy-start(bf16[512,1024]{1,0:T(8,128)(2,1)} %wout_hbm.1) | copy-start | bytes 3145732
  2.8 1.0 %copy-start.2 = (bf16[4,4,64,256]{3,2,1,0:T(8,128)(2,1)S(1)}, bf16[4,4,64,256]{3,2,1,0:T(8,128)(2,1)}, u32[]{:S(2)}) copy-start(bf16[4,4,64,256]{3,2,1,0:T(8,128)(2,1)} %kv_ref.1) | copy-start | bytes 1572868
  3.9 0.8 %copy-start.3 = (s32[4,2048]{1,0:T(4,128)S(1)}, s32[4,2048]{1,0:T(4,128)}, u32[]{:S(2)}) copy-start(s32[4,2048]{1,0:T(4,128)} %cand_ref.1) | copy-start | bytes 98308
  4.6 0.8 %copy-start.4 = (bf16[16,1024]{1,0:T(8,128)(2,1)S(1)}, bf16[16,1024]{1,0:T(8,128)(2,1)}, u32[]{:S(2)}) copy-start(bf16[16,1024]{1,0:T(8,128)(2,1)} %pool_ref.1) | copy-start | bytes 98308
  5.4 0.7 %copy-start.5 = (s32[4,16]{1,0:T(4,128)S(1)}, s32[4,16]{1,0:T(4,128)}, u32[]{:S(2)}) copy-start(s32[4,16]{1,0:T(4,128)} %slots_ref.1) | copy-start | bytes 772
  6.1 0.7 %copy-start.6 = (f32[512]{0:T(512)S(1)}, f32[512]{0:T(512)}, u32[]{:S(2)}) copy-start(f32[512]{0:T(512)} %param.13) | copy-start | bytes 6148
  6.7 0.7 %copy-start.7 = (s32[4]{0:T(128)S(1)}, s32[4]{0:T(128)}, u32[]{:S(2)}) copy-start(s32[4]{0:T(128)} %ranker_ref.1) | copy-start | bytes 52
  7.4 0.7 %copy-start.8 = (s32[4]{0:T(128)S(1)}, s32[4]{0:T(128)}, u32[]{:S(2)}) copy-start(s32[4]{0:T(128)} %blocks_ref.1) | copy-start | bytes 52

commit v2 on v1

--- a/solution.py
+++ b/solution.py
@@ -128,16 +128,22 @@
 
 def item_kernel(
     devices,
+    slots_hbm,
+    ranker_hbm,
+    blocks_hbm,
+    cand_hbm,
+    gain_hbm,
+    pool_hbm,
+    kv_hbm,
+    wqu_hbm,
+    wout_hbm,
+    out_ref,
     slots_ref,
     ranker_ref,
     blocks_ref,
     cand_ref,
     gain_ref,
-    pool_ref,
     kv_ref,
-    wqu_hbm,
-    wout_hbm,
-    out_ref,
     items,
     picked,
     history,
@@ -167,7 +173,7 @@
     slots_here, head_count, block_len, pair_width = kv_ref.shape
     head_dim = pair_width // 2
     user_count, most_blocks = slots_ref.shape
-    rows_here, model_width = pool_ref.shape
+    rows_here, model_width = pool_hbm.shape
     item_count = devices * rows_here
     half_items = item_count // 2
     share_rows = out_ref.shape[0]
@@ -189,10 +195,30 @@
     share = me % team
     core = bit_of(0)
 
-    load_qu = pltpu.make_async_copy(wqu_hbm, wqu, load_sem.at[0])
-    load_out = pltpu.make_async_copy(wout_hbm, wout, load_sem.at[1])
-    load_qu.start()
-    load_out.start()
+    place = 0
+    for j in range(bits):
+        place = place + bit_of(j) * (1 << (bits - 1 - j))
+
+    loads = [
+        pltpu.make_async_copy(source, target, load_sem.at[i])
+        for i, (source, target) in enumerate(
+            (
+                (slots_hbm, slots_ref),
+                (ranker_hbm, ranker_ref),
+                (blocks_hbm, blocks_ref),
+                (pool_hbm, items.at[place]),
+                (kv_hbm, kv_ref),
+                (cand_hbm, cand_ref),
+                (gain_hbm, gain_ref),
+                (wqu_hbm, wqu),
+                (wout_hbm, wout),
+            )
+        )
+    ]
+    for load in loads:
+        load.start()
+    load_slots, load_ranker, load_blocks, load_pool, load_kv = loads[:5]
+    load_cand, load_gain, load_qu, load_out = loads[5:]
 
     barrier = pltpu.get_barrier_semaphore()
     masks = [1, 2] + [team * d for d in range(1, user_count)]
@@ -201,10 +227,9 @@
             barrier, inc=1, device_id={"rank": flipped(mask)}, device_id_type=MESH
         )
 
-    place = 0
-    for j in range(bits):
-        place = place + bit_of(j) * (1 << (bits - 1 - j))
-    items[place] = pool_ref[...]
+    load_slots.wait()
+    load_ranker.wait()
+    load_blocks.wait()
     held, alive = [], []
     for u in range(user_count):
         slot, live = jnp.int32(0), jnp.int32(0)
@@ -215,15 +240,6 @@
             live = jnp.where(mine & (b < blocks_ref[u]), 1, live)
         held.append(slot)
         alive.append(live)
-    for g in range(user_count):
-        slot, live = jnp.int32(0), jnp.int32(0)
-        for u in range(user_count):
-            here = ranker_ref[u] == g
-            slot = jnp.where(here, held[u], slot)
-            live = jnp.where(here, alive[u], live)
-        block = kv_ref[slot]
-        picked[g] = jnp.where(live == 1, block, jnp.zeros_like(block))
-
     pl.semaphore_wait(barrier, len(masks))
 
     def pool_step(j):
@@ -239,26 +255,48 @@
         )
 
     def kv_copy(h, d):
-        other = flipped(team * d)
         return pltpu.make_async_remote_copy(
-            src_ref=picked.at[other // team, h],
+            src_ref=picked.at[d - 1, h],
             dst_ref=history.at[h, d],
             send_sem=kv_send.at[h, d - 1],
             recv_sem=kv_recv.at[h, d - 1],
-            device_id={"rank": other},
+            device_id={"rank": flipped(team * d)},
             device_id_type=MESH,
         )
 
+    far_first = range(user_count - 1, 0, -1)
+
+    def send_head(h):
+        for d in far_first:
+            kv_copy(h, d).start()
+
+    load_pool.wait()
     pool_step(bits - 1).start()
-    kv_copies = {}
-    for h in range(head_count):
-        for d in reversed(range(1, user_count)):
-            kv_copies[h, d] = kv_copy(h, d)
-            kv_copies[h, d].start()
-
-    for h in range(head_count):
-        history[h, 0] = picked[my_group, h]
-
+
+    load_kv.wait()
+    for d in (*far_first, 0):
+        group = flipped(team * d) // team
+        slot, live = jnp.int32(0), jnp.int32(0)
+        for u in range(user_count):
+            here = ranker_ref[u] == group
+            slot = jnp.where(here, held[u], slot)
+            live = jnp.where(here, alive[u], live)
+        block = kv_ref[slot]
+        block = jnp.where(live == 1, block, jnp.zeros_like(block))
+        if d > 0:
+            picked[d - 1] = block
+            kv_copy(0, d).start()
+        else:
+            history[:, 0] = block
+
+    waves = list(range(1, head_count))
+    for j in range(bits - 1, 1, -1):
+        pool_step(j).wait()
+        pool_step(j - 1).start()
+        if waves:
+            send_head(waves.pop(0))
+
+    load_cand.wait()
     first = pl.multiple_of(share * share_rows, share_rows)
     ids = jnp.zeros((1, share_rows), jnp.int32)
     for u in range(user_count):
@@ -272,24 +310,29 @@
     hits = (item_at == ids).astype(jnp.float32)
     onehot[...] = hits.T.astype(jnp.bfloat16)
 
-    for j in reversed(range(bits)):
-        step = pool_step(j)
-        if j < bits - 1:
-            step.start()
-        step.wait()
-
+    half_blocks = devices // 2
     load_qu.wait()
-    all_items = items[...].reshape(item_count, model_width)
-    for h in range(head_count):
-        qu = jnp.dot(
-            all_items,
-            wqu[:, h * pair_width : (h + 1) * pair_width],
-            preferred_element_type=jnp.float32,
-        )
-        head_qu[h] = silu(qu).astype(jnp.bfloat16)
+
+    def project_in(at, block_from):
+        some = items[pl.ds(block_from, half_blocks)].reshape(half_items, model_width)
+        for h in range(head_count):
+            qu = jnp.dot(
+                some,
+                wqu[:, h * pair_width : (h + 1) * pair_width],
+                preferred_element_type=jnp.float32,
+            )
+            head_qu[h, pl.ds(at, half_items)] = silu(qu).astype(jnp.bfloat16)
 
     mine_at = pl.multiple_of(core * half_items, half_items)
     other_at = pl.multiple_of((1 - core) * half_items, half_items)
+
+    pool_step(1).wait()
+    pool_step(0).start()
+    for h in waves:
+        send_head(h)
+    project_in(mine_at, core * half_blocks)
+    pool_step(0).wait()
+    project_in(other_at, (1 - core) * half_blocks)
 
     def core_copy(h):
         return pltpu.make_async_remote_copy(
@@ -318,7 +361,7 @@
 
     for h in range(head_count):
         for d in range(1, user_count):
-            kv_copies[h, d].wait()
+            kv_copy(h, d).wait()
         pairs = history[h].reshape(user_count * block_len, pair_width)
         scores = lax.dot_general(
             head_qu[h, :, :head_dim],
@@ -341,6 +384,7 @@
     mean = sum(jnp.sum(a, axis=1, keepdims=True) for a in attended) / width
     square = sum(jnp.sum(a * a, axis=1, keepdims=True) for a in attended) / width
     scale = lax.rsqrt(square - mean * mean + norm_eps)
+    load_gain.wait()
     for h in range(head_count):
         columns = slice(h * head_dim, (h + 1) * head_dim)
         gate = head_qu[h, pl.ds(mine_at, half_items), head_dim:].astype(jnp.float32)
@@ -359,8 +403,6 @@
     swap.start()
     load_out.wait()
 
-    half_blocks = devices // 2
-
     def project(at, block_from):
         base = items[pl.ds(block_from, half_blocks)].reshape(half_items, model_width)
         mixed = base.astype(jnp.float32) + jnp.dot(
@@ -387,19 +429,24 @@
     share_rows = cand_ids.shape[1] * user_count // devices
     width = head_count * head_dim
     bits = devices.bit_length() - 1
-    smem = pl.BlockSpec(memory_space=pltpu.SMEM)
     vmem = pl.BlockSpec(memory_space=pltpu.VMEM)
-    hbm = pl.BlockSpec(memory_space=pl.ANY)
+    hbm = pl.BlockSpec(memory_space=pltpu.HBM)
     dma = pltpu.SemaphoreType.DMA
     narrow, wide = jnp.bfloat16, jnp.float32
     return pl.pallas_call(
         functools.partial(item_kernel, devices),
         out_shape=jax.ShapeDtypeStruct((share_rows, model_width), narrow),
-        in_specs=[smem, smem, smem, vmem, vmem, vmem, vmem, hbm, hbm],
+        in_specs=[hbm] * 9,
         out_specs=vmem,
         scratch_shapes=[
+            pltpu.SMEM(cache_slot.shape, jnp.int32),
+            pltpu.SMEM(ranker.shape, jnp.int32),
+            pltpu.SMEM(hist_blocks.shape, jnp.int32),
+            pltpu.VMEM(cand_ids.shape, jnp.int32),
+            pltpu.VMEM((1, width), wide),
+            pltpu.VMEM(kv_cache.shape, narrow),
             pltpu.VMEM((devices, rows_here, model_width), narrow),
-            pltpu.VMEM((user_count, head_count, block_len, pair_width), narrow),
+            pltpu.VMEM((user_count - 1, head_count, block_len, pair_width), narrow),
             pltpu.VMEM((head_count, user_count, block_len, pair_width), narrow),
             pltpu.VMEM(w_qu.shape, narrow),
             pltpu.VMEM(w_out.shape, narrow),
@@ -411,7 +458,7 @@
             pltpu.VMEM((item_count, width), narrow),
             pltpu.VMEM((item_count, model_width), narrow),
             pltpu.VMEM((share_rows, item_count), narrow),
-            dma((2,)),
+            dma((9,)),
             dma((bits,)),
             dma((bits,)),
             dma((head_count, user_count - 1)),
@@ -424,7 +471,7 @@
             dma,
         ],
         compiler_params=pltpu.CompilerParams(
-            collective_id=0, has_side_effects=True, vmem_limit_bytes=40 * 1024 * 1024
+            collective_id=0, has_side_effects=True, vmem_limit_bytes=62 * 1024 * 1024
         ),
     )(
         cache_slot,

time: 43.4 us -> 33.1 us (0.76)
  local copies, waits for them, and re-layouts: 9.01 us -> 2.26 us
  Pallas kernels: 34 us -> 30.7 us
    unnamed x19 -> x1, local copies, waits for them, and re-layouts: 9.01 us -> 2.26 us
    pallas_call x1, Pallas kernels: 34 us -> 30.7 us  [item_body(): pl.pallas_call(functools.partial(item_kernel, devices), out_shape=jax.Sha...]
where the time goes in v2:
time: 33.1 us; the launch traced here: 32.9 us
  Pallas kernels  30.7 us (93%)
  local copies, waits for them, and re-layouts  2.26 us (7%)
    pallas_call x1, Pallas kernels, item_body(): pl.pallas_call(functools.partial(item_kernel, devices), out_shape=jax.Sha...  30.7 us
    unnamed x1, local copies, waits for them, and re-layouts  2.26 us

profile of v2, /device:TPU:0, one launch (start us, length us, event | category | flops | bytes accessed | tf_op | source)
XLA Modules:
  0.0 32.9 jit_solution(14713509476158089173)
XLA Ops:
  0.0 30.7 %shard_map.91 = bf16[512,1024]{1,0:T(8,128)(2,1)} custom-call(s32[4,16]{1,0:T(4,128)} %slots_hbm.1, s32[4]{0:T(128)} %ranker_hbm.1, s32[4]{0:T(128)} %blocks_hbm.1, s32[4,2048]{1,0:T(4,128)} %cand_hbm.1, f32[1,512]{1,0:T(1,128)} %bitcast.1, bf16[16,1024]{1,0:T(8,128)(2,1)} %pool_hbm.1, bf16[4,4,64,256]{3,2,1,0:T(8,128)(2,1)} %kv_hbm.1, ...), custom_call_target="tpu_custom_call" | custom-call | tf_op jit(solution)/shard_map/pallas_call | solution.py:436
  30.7 2.3 %copy.11 = bf16[512,1024]{1,0:T(8,128)(2,1)} copy(bf16[512,1024]{1,0:T(8,128)(2,1)} %shard_map.91) | data formatting | bytes 2097152

commit v3 on v2

--- a/solution.py
+++ b/solution.py
@@ -137,7 +137,8 @@
     kv_hbm,
     wqu_hbm,
     wout_hbm,
-    out_ref,
+    table_hbm,
+    onehot_hbm,
     slots_ref,
     ranker_ref,
     blocks_ref,
@@ -153,11 +154,13 @@
     partial,
     core_in,
     chip_sum,
+    chip_out,
     chip_in,
     hidden,
     table,
     onehot,
     load_sem,
+    store_sem,
     pool_send,
     pool_recv,
     kv_send,
@@ -176,13 +179,15 @@
     rows_here, model_width = pool_hbm.shape
     item_count = devices * rows_here
     half_items = item_count // 2
-    share_rows = out_ref.shape[0]
+    share_rows = onehot_hbm.shape[0]
     team = devices // user_count
     bits = devices.bit_length() - 1
     score_scale = 1.0 / math.sqrt(head_dim)
 
+    my_bits = [lax.rem(lax.div(me, 1 << j), 2) for j in range(bits)]
+
     def bit_of(j):
-        return (me // (1 << j)) % 2
+        return my_bits[j]
 
     def flipped(mask):
         other = me
@@ -191,8 +196,8 @@
                 other = other + (1 << j) * (1 - 2 * bit_of(j))
         return other
 
-    my_group = me // team
-    share = me % team
+    my_group = lax.div(me, team)
+    share = lax.rem(me, team)
     core = bit_of(0)
 
     place = 0
@@ -230,13 +235,15 @@
     load_slots.wait()
     load_ranker.wait()
     load_blocks.wait()
+    first_slot = me * slots_here
     held, alive = [], []
     for u in range(user_count):
         slot, live = jnp.int32(0), jnp.int32(0)
         for b in range(most_blocks):
             entry = slots_ref[u, b]
-            mine = lax.div(entry, slots_here) == me
-            slot = jnp.where(mine, lax.rem(entry, slots_here), slot)
+            offset = entry - first_slot
+            mine = (offset >= 0) & (offset < slots_here)
+            slot = jnp.where(mine, offset, slot)
             live = jnp.where(mine & (b < blocks_ref[u]), 1, live)
         held.append(slot)
         alive.append(live)
@@ -244,7 +251,7 @@
 
     def pool_step(j):
         span = 1 << (bits - 1 - j)
-        part = items.at[pl.ds((place // span) * span, span)]
+        part = items.at[pl.ds(lax.div(place, span) * span, span)]
         return pltpu.make_async_remote_copy(
             src_ref=part,
             dst_ref=part,
@@ -275,7 +282,7 @@
 
     load_kv.wait()
     for d in (*far_first, 0):
-        group = flipped(team * d) // team
+        group = lax.div(flipped(team * d), team)
         slot, live = jnp.int32(0), jnp.int32(0)
         for u in range(user_count):
             here = ranker_ref[u] == group
@@ -301,14 +308,14 @@
     ids = jnp.zeros((1, share_rows), jnp.int32)
     for u in range(user_count):
         ids = jnp.where(ranker_ref[u] == my_group, cand_ref[pl.ds(u, 1), pl.ds(first, share_rows)], ids)
-    row = lax.broadcasted_iota(jnp.int32, (item_count, share_rows), 0)
-    block_at = row // rows_here
-    rank_at = jnp.zeros_like(row)
-    for j in range(bits):
-        rank_at = rank_at + ((block_at >> j) & 1) * (1 << (bits - 1 - j))
-    item_at = rank_at * rows_here + row % rows_here
-    hits = (item_at == ids).astype(jnp.float32)
-    onehot[...] = hits.T.astype(jnp.bfloat16)
+    row = lax.broadcasted_iota(jnp.int32, (rows_here, share_rows), 0)
+    hits = []
+    for at in range(devices):
+        rank_at = sum((at >> j & 1) << bits - 1 - j for j in range(bits))
+        hits.append((row + rank_at * rows_here == ids).astype(jnp.float32))
+    onehot[...] = jnp.concatenate(hits, axis=0).T.astype(jnp.bfloat16)
+    store_onehot = pltpu.make_async_copy(onehot, onehot_hbm, store_sem.at[0])
+    store_onehot.start()
 
     half_blocks = devices // 2
     load_qu.wait()
@@ -346,7 +353,7 @@
 
     def chip_copy(h):
         return pltpu.make_async_remote_copy(
-            src_ref=chip_sum.at[h],
+            src_ref=chip_out.at[h],
             dst_ref=chip_in.at[h],
             send_sem=chip_send.at[h],
             recv_sem=chip_recv.at[h],
@@ -357,34 +364,43 @@
     def to_chip(h):
         core_copy(h).wait()
         chip_sum[h] = partial[h, pl.ds(mine_at, half_items)] + core_in[h]
+        chip_out[h] = chip_sum[h].astype(jnp.bfloat16)
         chip_copy(h).start()
 
     for h in range(head_count):
         for d in range(1, user_count):
             kv_copy(h, d).wait()
         pairs = history[h].reshape(user_count * block_len, pair_width)
-        scores = lax.dot_general(
-            head_qu[h, :, :head_dim],
-            pairs[:, :head_dim],
-            (((1,), (1,)), ((), ())),
-            preferred_element_type=jnp.float32,
-        )
-        weights = silu(scores * score_scale).astype(jnp.bfloat16)
-        partial[h] = jnp.dot(weights, pairs[:, head_dim:], preferred_element_type=jnp.float32)
-        core_copy(h).start()
+        for at in (other_at, mine_at):
+            scores = lax.dot_general(
+                head_qu[h, pl.ds(at, half_items), :head_dim],
+                pairs[:, :head_dim],
+                (((1,), (1,)), ((), ())),
+                preferred_element_type=jnp.float32,
+            )
+            weights = silu(scores * score_scale).astype(jnp.bfloat16)
+            partial[h, pl.ds(at, half_items)] = jnp.dot(
+                weights, pairs[:, head_dim:], preferred_element_type=jnp.float32
+            )
+            if at is other_at:
+                core_copy(h).start()
         if h > 0:
             to_chip(h - 1)
     to_chip(head_count - 1)
 
-    attended = []
+    load_gain.wait()
+    load_out.wait()
+    width = head_count * head_dim
+    attended, mean, square = [], 0.0, 0.0
     for h in range(head_count):
         chip_copy(h).wait()
-        attended.append(chip_sum[h] + chip_in[h])
-    width = head_count * head_dim
-    mean = sum(jnp.sum(a, axis=1, keepdims=True) for a in attended) / width
-    square = sum(jnp.sum(a * a, axis=1, keepdims=True) for a in attended) / width
+        one = chip_sum[h] + chip_in[h].astype(jnp.float32)
+        mean = mean + jnp.sum(one, axis=1, keepdims=True)
+        square = square + jnp.sum(one * one, axis=1, keepdims=True)
+        attended.append(one)
+    mean = mean / width
+    square = square / width
     scale = lax.rsqrt(square - mean * mean + norm_eps)
-    load_gain.wait()
     for h in range(head_count):
         columns = slice(h * head_dim, (h + 1) * head_dim)
         gate = head_qu[h, pl.ds(mine_at, half_items), head_dim:].astype(jnp.float32)
@@ -401,7 +417,6 @@
         device_id_type=MESH,
     )
     swap.start()
-    load_out.wait()
 
     def project(at, block_from):
         base = items[pl.ds(block_from, half_blocks)].reshape(half_items, model_width)
@@ -410,12 +425,18 @@
         )
         table[pl.ds(at, half_items)] = mixed.astype(jnp.bfloat16)
 
+    def store_half(at, i):
+        part = pl.ds(at, half_items)
+        return pltpu.make_async_copy(table.at[part], table_hbm.at[part], store_sem.at[i])
+
     project(mine_at, core * half_blocks)
+    store_half(mine_at, 1).start()
     swap.wait()
     project(other_at, (1 - core) * half_blocks)
-    out_ref[...] = jnp.dot(
-        onehot[...], table[...], preferred_element_type=jnp.float32
-    ).astype(jnp.bfloat16)
+    store_half(other_at, 2).start()
+    store_onehot.wait()
+    store_half(mine_at, 1).wait()
+    store_half(other_at, 2).wait()
 
 
 def item_body(pool, kv_cache, w_qu, w_out, norm_gain, cand_ids, ranker, hist_blocks, cache_slot):
@@ -429,15 +450,17 @@
     share_rows = cand_ids.shape[1] * user_count // devices
     width = head_count * head_dim
     bits = devices.bit_length() - 1
-    vmem = pl.BlockSpec(memory_space=pltpu.VMEM)
     hbm = pl.BlockSpec(memory_space=pltpu.HBM)
     dma = pltpu.SemaphoreType.DMA
     narrow, wide = jnp.bfloat16, jnp.float32
-    return pl.pallas_call(
+    table, onehot = pl.pallas_call(
         functools.partial(item_kernel, devices),
-        out_shape=jax.ShapeDtypeStruct((share_rows, model_width), narrow),
+        out_shape=(
+            jax.ShapeDtypeStruct((item_count, model_width), narrow),
+            jax.ShapeDtypeStruct((share_rows, item_count), narrow),
+        ),
         in_specs=[hbm] * 9,
-        out_specs=vmem,
+        out_specs=(hbm, hbm),
         scratch_shapes=[
             pltpu.SMEM(cache_slot.shape, jnp.int32),
             pltpu.SMEM(ranker.shape, jnp.int32),
@@ -454,11 +477,13 @@
             pltpu.VMEM((head_count, item_count, head_dim), wide),
             pltpu.VMEM((head_count, half_items, head_dim), wide),
             pltpu.VMEM((head_count, half_items, head_dim), wide),
-            pltpu.VMEM((head_count, half_items, head_dim), wide),
+            pltpu.VMEM((head_count, half_items, head_dim), narrow),
+            pltpu.VMEM((head_count, half_items, head_dim), narrow),
             pltpu.VMEM((item_count, width), narrow),
             pltpu.VMEM((item_count, model_width), narrow),
             pltpu.VMEM((share_rows, item_count), narrow),
             dma((9,)),
+            dma((3,)),
             dma((bits,)),
             dma((bits,)),
             dma((head_count, user_count - 1)),
@@ -484,6 +509,7 @@
         w_qu,
         w_out,
     )
+    return jnp.dot(onehot, table, preferred_element_type=wide).astype(narrow)
 
 
 def body(pool, kv_cache, w_qu, w_out, norm_gain, cand_ids, ranker, hist_blocks, cache_slot):

time: 33.1 us -> 31.6 us (0.955)
  matrix products: 0 us -> 2.54 us
  local copies, waits for them, and re-layouts: 2.26 us -> 0 us
  Pallas kernels: 30.7 us -> 28.8 us
    dot_general x0 -> x1, matrix products: none -> 2.54 us  [item_body(): return jnp.dot(onehot, table, preferred_element_type=wide).astype(narrow)]
    unnamed x1 -> x0, local copies, waits for them, and re-layouts: 2.26 us -> none
    pallas_call x1, Pallas kernels: 30.7 us -> 28.8 us  [item_body(): pl.pallas_call(functools.partial(item_kernel, devices), out_shape=(jax.Sh...]
where the time goes in v3:
time: 31.6 us; the launch traced here: 31.4 us
  Pallas kernels  28.8 us (91%)
  matrix products  2.54 us (8%)
    pallas_call x1, Pallas kernels, item_body(): pl.pallas_call(functools.partial(item_kernel, devices), out_shape=(jax.Sh...  28.8 us
    dot_general x1, matrix products, item_body(): return jnp.dot(onehot, table, preferred_element_type=wide).astype(narrow)  2.54 us

profile of v3, /device:TPU:0, one launch (start us, length us, event | category | flops | bytes accessed | tf_op | source)
XLA Modules:
  0.0 31.4 jit_solution(8980121945120348432)
XLA Ops:
  0.0 28.8 %shard_map.91 = (bf16[256,1024]{1,0:T(8,128)(2,1)}, bf16[512,256]{1,0:T(8,128)(2,1)}) custom-call(s32[4,16]{1,0:T(4,128)} %slots_hbm.1, s32[4]{0:T(128)} %ranker_hbm.1, s32[4]{0:T(128)} %blocks_hbm.1, s32[4,2048]{1,0:T(4,128)} %cand_hbm.1, f32[1,512]{1,0:T(1,128)} %bitcast.3, bf16[16,1024]{1,0:T(8,128)(2,1)} %pool_hbm.1, bf16[4,4,64,256]{3,2,1,0:T(8,128)(2,1)} %kv_hbm.1, ...), custom_call_target="tpu_custom_call" | custom-call | tf_op jit(solution)/shard_map/pallas_call | solution.py:456
  28.9 2.5 %convolution_convert_fusion = bf16[512,1024]{1,0:T(8,128)(2,1)} fusion(bf16[512,256]{1,0:T(8,128)(2,1)} %get-tuple-element.7, bf16[256,1024]{1,0:T(8,128)(2,1)} %get-tuple-element.8), kind=kOutput, calls=%fused_computation | convolution fusion | flops 268959744 | bytes 1835008 | tf_op jit(solution)/shard_map/dot_general | solution.py:512

commit v4 on v3

--- a/solution.py
+++ b/solution.py
@@ -137,8 +137,7 @@
     kv_hbm,
     wqu_hbm,
     wout_hbm,
-    table_hbm,
-    onehot_hbm,
+    out_ref,
     slots_ref,
     ranker_ref,
     blocks_ref,
@@ -157,10 +156,8 @@
     chip_out,
     chip_in,
     hidden,
-    table,
     onehot,
     load_sem,
-    store_sem,
     pool_send,
     pool_recv,
     kv_send,
@@ -179,7 +176,7 @@
     rows_here, model_width = pool_hbm.shape
     item_count = devices * rows_here
     half_items = item_count // 2
-    share_rows = onehot_hbm.shape[0]
+    share_rows = out_ref.shape[0]
     team = devices // user_count
     bits = devices.bit_length() - 1
     score_scale = 1.0 / math.sqrt(head_dim)
@@ -292,16 +289,17 @@
         block = jnp.where(live == 1, block, jnp.zeros_like(block))
         if d > 0:
             picked[d - 1] = block
-            kv_copy(0, d).start()
         else:
             history[:, 0] = block
 
-    waves = list(range(1, head_count))
+    waves = list(range(head_count))
     for j in range(bits - 1, 1, -1):
         pool_step(j).wait()
         pool_step(j - 1).start()
         if waves:
             send_head(waves.pop(0))
+    if waves:
+        send_head(waves.pop(0))
 
     load_cand.wait()
     first = pl.multiple_of(share * share_rows, share_rows)
@@ -313,9 +311,9 @@
     for at in range(devices):
         rank_at = sum((at >> j & 1) << bits - 1 - j for j in range(bits))
         hits.append((row + rank_at * rows_here == ids).astype(jnp.float32))
-    onehot[...] = jnp.concatenate(hits, axis=0).T.astype(jnp.bfloat16)
-    store_onehot = pltpu.make_async_copy(onehot, onehot_hbm, store_sem.at[0])
-    store_onehot.start()
+    for half in range(2):
+        some = jnp.concatenate(hits[half * devices // 2 : (half + 1) * devices // 2], axis=0)
+        onehot[half] = some.T.astype(jnp.bfloat16)
 
     half_blocks = devices // 2
     load_qu.wait()
@@ -418,25 +416,18 @@
     )
     swap.start()
 
-    def project(at, block_from):
-        base = items[pl.ds(block_from, half_blocks)].reshape(half_items, model_width)
+    def select(at, half):
+        base = items[pl.ds(half * half_blocks, half_blocks)].reshape(half_items, model_width)
         mixed = base.astype(jnp.float32) + jnp.dot(
             hidden[pl.ds(at, half_items)], wout[...], preferred_element_type=jnp.float32
         )
-        table[pl.ds(at, half_items)] = mixed.astype(jnp.bfloat16)
-
-    def store_half(at, i):
-        part = pl.ds(at, half_items)
-        return pltpu.make_async_copy(table.at[part], table_hbm.at[part], store_sem.at[i])
-
-    project(mine_at, core * half_blocks)
-    store_half(mine_at, 1).start()
+        return jnp.dot(
+            onehot[half], mixed.astype(jnp.bfloat16), preferred_element_type=jnp.float32
+        ).astype(jnp.bfloat16)
+
+    out_ref[...] = select(mine_at, core)
     swap.wait()
-    project(other_at, (1 - core) * half_blocks)
-    store_half(other_at, 2).start()
-    store_onehot.wait()
-    store_half(mine_at, 1).wait()
-    store_half(other_at, 2).wait()
+    out_ref[...] = out_ref[...] + select(other_at, 1 - core)
 
 
 def item_body(pool, kv_cache, w_qu, w_out, norm_gain, cand_ids, ranker, hist_blocks, cache_slot):
@@ -453,14 +444,11 @@
     hbm = pl.BlockSpec(memory_space=pltpu.HBM)
     dma = pltpu.SemaphoreType.DMA
     narrow, wide = jnp.bfloat16, jnp.float32
-    table, onehot = pl.pallas_call(
+    return pl.pallas_call(
         functools.partial(item_kernel, devices),
-        out_shape=(
-            jax.ShapeDtypeStruct((item_count, model_width), narrow),
-            jax.ShapeDtypeStruct((share_rows, item_count), narrow),
-        ),
+        out_shape=jax.ShapeDtypeStruct((share_rows, model_width), narrow),
         in_specs=[hbm] * 9,
-        out_specs=(hbm, hbm),
+        out_specs=pl.BlockSpec(memory_space=pltpu.VMEM),
         scratch_shapes=[
             pltpu.SMEM(cache_slot.shape, jnp.int32),
             pltpu.SMEM(ranker.shape, jnp.int32),
@@ -480,10 +468,8 @@
             pltpu.VMEM((head_count, half_items, head_dim), narrow),
             pltpu.VMEM((head_count, half_items, head_dim), narrow),
             pltpu.VMEM((item_count, width), narrow),
-            pltpu.VMEM((item_count, model_width), narrow),
-            pltpu.VMEM((share_rows, item_count), narrow),
+            pltpu.VMEM((2, share_rows, half_items), narrow),
             dma((9,)),
-            dma((3,)),
             dma((bits,)),
             dma((bits,)),
             dma((head_count, user_count - 1)),
@@ -509,7 +495,6 @@
         w_qu,
         w_out,
     )
-    return jnp.dot(onehot, table, preferred_element_type=wide).astype(narrow)
 
 
 def body(pool, kv_cache, w_qu, w_out, norm_gain, cand_ids, ranker, hist_blocks, cache_slot):

time: 31.6 us -> 31.6 us (level)
  matrix products: 2.54 us -> 0 us
  local copies, waits for them, and re-layouts: 0 us -> 2.26 us
  Pallas kernels: 28.8 us -> 29.2 us
    dot_general x1 -> x0, matrix products: 2.54 us -> none  [item_body(): return jnp.dot(onehot, table, preferred_element_type=wide).astype(narrow)]
    unnamed x0 -> x1, local copies, waits for them, and re-layouts: none -> 2.26 us
    pallas_call x1, Pallas kernels: 28.8 us -> 29.2 us  [item_body(): pl.pallas_call(functools.partial(item_kernel, devices), out_shape=jax.Sha...]
where the time goes in v4:
time: 31.6 us; the launch traced here: 31.5 us
  Pallas kernels  29.2 us (92%)
  local copies, waits for them, and re-layouts  2.26 us (7%)
    pallas_call x1, Pallas kernels, item_body(): pl.pallas_call(functools.partial(item_kernel, devices), out_shape=jax.Sha...  29.2 us
    unnamed x1, local copies, waits for them, and re-layouts  2.26 us

profile of v4, /device:TPU:0, one launch (start us, length us, event | category | flops | bytes accessed | tf_op | source)
XLA Modules:
  0.0 31.5 jit_solution(15862759896586489176)
XLA Ops:
  0.0 29.2 %shard_map.91 = bf16[512,1024]{1,0:T(8,128)(2,1)} custom-call(s32[4,16]{1,0:T(4,128)} %slots_hbm.1, s32[4]{0:T(128)} %ranker_hbm.1, s32[4]{0:T(128)} %blocks_hbm.1, s32[4,2048]{1,0:T(4,128)} %cand_hbm.1, f32[1,512]{1,0:T(1,128)} %bitcast.1, bf16[16,1024]{1,0:T(8,128)(2,1)} %pool_hbm.1, bf16[4,4,64,256]{3,2,1,0:T(8,128)(2,1)} %kv_hbm.1, ...), custom_call_target="tpu_custom_call" | custom-call | tf_op jit(solution)/shard_map/pallas_call | solution.py:447
  29.2 2.3 %copy.11 = bf16[512,1024]{1,0:T(8,128)(2,1)} copy(bf16[512,1024]{1,0:T(8,128)(2,1)} %shard_map.91) | data formatting | bytes 2097152

commit v5 on v3

--- a/solution.py
+++ b/solution.py
@@ -437,6 +437,12 @@
     store_onehot.wait()
     store_half(mine_at, 1).wait()
     store_half(other_at, 2).wait()
+
+
+def select_kernel(onehot_ref, table_ref, out_ref):
+    out_ref[...] = jnp.dot(
+        onehot_ref[...], table_ref[...], preferred_element_type=jnp.float32
+    ).astype(jnp.bfloat16)
 
 
 def item_body(pool, kv_cache, w_qu, w_out, norm_gain, cand_ids, ranker, hist_blocks, cache_slot):
@@ -509,7 +515,18 @@
         w_qu,
         w_out,
     )
-    return jnp.dot(onehot, table, preferred_element_type=wide).astype(narrow)
+    row_block = share_rows // 2
+    return pl.pallas_call(
+        select_kernel,
+        grid=(2,),
+        out_shape=jax.ShapeDtypeStruct((share_rows, model_width), narrow),
+        in_specs=[
+            pl.BlockSpec((row_block, item_count), lambda i: (i, 0)),
+            pl.BlockSpec((item_count, model_width), lambda i: (0, 0)),
+        ],
+        out_specs=pl.BlockSpec((row_block, model_width), lambda i: (i, 0)),
+        compiler_params=pltpu.CompilerParams(vmem_limit_bytes=62 * 1024 * 1024),
+    )(onehot, table)
 
 
 def body(pool, kv_cache, w_qu, w_out, norm_gain, cand_ids, ranker, hist_blocks, cache_slot):

time: 31.6 us -> 31.6 us (level)
  Pallas kernels: 28.8 us -> 31.4 us
  matrix products: 2.54 us -> 0 us
    pallas_call x0 -> x1, Pallas kernels: none -> 2.55 us  [item_body(): pl.pallas_call(select_kernel, grid=(2,), out_shape=jax.ShapeDtypeStruct((...]
    dot_general x1 -> x0, matrix products: 2.54 us -> none  [item_body(): return jnp.dot(onehot, table, preferred_element_type=wide).astype(narrow)]
where the time goes in v5:
time: 31.6 us; the launch traced here: 31.4 us
  Pallas kernels  31.4 us (99%)
    pallas_call x1, Pallas kernels, item_body(): pl.pallas_call(functools.partial(item_kernel, devices), out_shape=(jax.Sh...  28.8 us
    pallas_call x1, Pallas kernels, item_body(): pl.pallas_call(select_kernel, grid=(2,), out_shape=jax.ShapeDtypeStruct((...  2.55 us

profile of v5, /device:TPU:0, one launch (start us, length us, event | category | flops | bytes accessed | tf_op | source)
XLA Modules:
  0.0 31.4 jit_solution(9949464528388241866)
XLA Ops:
  0.0 28.8 %shard_map.91 = (bf16[256,1024]{1,0:T(8,128)(2,1)}, bf16[512,256]{1,0:T(8,128)(2,1)}) custom-call(s32[4,16]{1,0:T(4,128)} %slots_hbm.1, s32[4]{0:T(128)} %ranker_hbm.1, s32[4]{0:T(128)} %blocks_hbm.1, s32[4,2048]{1,0:T(4,128)} %cand_hbm.1, f32[1,512]{1,0:T(1,128)} %bitcast.1, bf16[16,1024]{1,0:T(8,128)(2,1)} %pool_hbm.1, bf16[4,4,64,256]{3,2,1,0:T(8,128)(2,1)} %kv_hbm.1, ...), custom_call_target="tpu_custom_call" | custom-call | tf_op jit(solution)/shard_map/pallas_call | solution.py:462
  28.9 2.5 %shard_map.92 = bf16[512,1024]{1,0:T(8,128)(2,1)} custom-call(bf16[512,256]{1,0:T(8,128)(2,1)} %get-tuple-element.7.onehot_ref, bf16[256,1024]{1,0:T(8,128)(2,1)} %get-tuple-element.8.table_ref), custom_call_target="tpu_custom_call" | custom-call | tf_op jit(solution)/shard_map/pallas_call | solution.py:519

commit v6 on v3

--- a/solution.py
+++ b/solution.py
@@ -296,12 +296,13 @@
         else:
             history[:, 0] = block
 
-    waves = list(range(1, head_count))
-    for j in range(bits - 1, 1, -1):
+    pool_step(bits - 1).wait()
+    pool_step(bits - 2).start()
+    for h in range(1, head_count):
+        send_head(h)
+    for j in range(bits - 2, 1, -1):
         pool_step(j).wait()
         pool_step(j - 1).start()
-        if waves:
-            send_head(waves.pop(0))
 
     load_cand.wait()
     first = pl.multiple_of(share * share_rows, share_rows)
@@ -335,8 +336,6 @@
 
     pool_step(1).wait()
     pool_step(0).start()
-    for h in waves:
-        send_head(h)
     project_in(mine_at, core * half_blocks)
     pool_step(0).wait()
     project_in(other_at, (1 - core) * half_blocks)

time: 31.6 us -> 30.8 us (0.975)
  Pallas kernels: 28.8 us -> 28.1 us
    pallas_call x1, Pallas kernels: 28.8 us -> 28.1 us  [item_body(): pl.pallas_call(functools.partial(item_kernel, devices), out_shape=(jax.Sh...]
where the time goes in v6:
time: 30.8 us; the launch traced here: 30.6 us
  Pallas kernels  28.1 us (91%)
  matrix products  2.54 us (8%)
    pallas_call x1, Pallas kernels, item_body(): pl.pallas_call(functools.partial(item_kernel, devices), out_shape=(jax.Sh...  28.1 us
    dot_general x1, matrix products, item_body(): return jnp.dot(onehot, table, preferred_element_type=wide).astype(narrow)  2.54 us

profile of v6, /device:TPU:0, one launch (start us, length us, event | category | flops | bytes accessed | tf_op | source)
XLA Modules:
  0.0 30.6 jit_solution(17927845888411144014)
XLA Ops:
  0.0 28.1 %shard_map.91 = (bf16[256,1024]{1,0:T(8,128)(2,1)}, bf16[512,256]{1,0:T(8,128)(2,1)}) custom-call(s32[4,16]{1,0:T(4,128)} %slots_hbm.1, s32[4]{0:T(128)} %ranker_hbm.1, s32[4]{0:T(128)} %blocks_hbm.1, s32[4,2048]{1,0:T(4,128)} %cand_hbm.1, f32[1,512]{1,0:T(1,128)} %bitcast.3, bf16[16,1024]{1,0:T(8,128)(2,1)} %pool_hbm.1, bf16[4,4,64,256]{3,2,1,0:T(8,128)(2,1)} %kv_hbm.1, ...), custom_call_target="tpu_custom_call" | custom-call | tf_op jit(solution)/shard_map/pallas_call | solution.py:455
  28.1 2.5 %convolution_convert_fusion = bf16[512,1024]{1,0:T(8,128)(2,1)} fusion(bf16[512,256]{1,0:T(8,128)(2,1)} %get-tuple-element.7, bf16[256,1024]{1,0:T(8,128)(2,1)} %get-tuple-element.8), kind=kOutput, calls=%fused_computation | convolution fusion | flops 268959744 | bytes 1835008 | tf_op jit(solution)/shard_map/dot_general | solution.py:511
